TPU v7x, 32 devices: a whole 2x2x4 slice. The times are simulated.
32 devices in a mesh: groups: 2 (over y), ex: 4 (over z), ey: 4 (over x, core).
Axes of the slice: x: 2, y: 2, z: 4, core: 2. Of those that a mesh axis runs over, the one named last changes fastest.
Arguments:
- tokens: bfloat16 [128, 7168], P(('groups', 'ex', 'ey')), parts along dimension 0, may hold values from -6 to 6
- route: int32 [128, 2], P(('groups', 'ex', 'ey')), parts along dimension 0, may hold values from 0 to 3, all different within a row; in each aligned block of 4 rows (0 to 3, 4 to 7, ...) at most 4 rows name the same one
- gates: float32 [128, 2], P(('groups', 'ex', 'ey')), parts along dimension 0, may hold values from 0.2 to 1.5
- w_gate: bfloat16 [4, 7168, 2048], P('ex', None, 'ey'), may hold values from -0.0625 to 0.0625
- w_up: bfloat16 [4, 7168, 2048], P('ex', None, 'ey'), may hold values from -0.0625 to 0.0625
- w_down: bfloat16 [4, 2048, 7168], P('ex', 'ey'), may hold values from -0.125 to 0.125
Outputs:
- mixed: bfloat16 [128, 7168], P(('groups', 'ex', 'ey')), parts along dimension 0
There are 2 independent parts, one for each index of `groups`. A program takes and returns all parts, laid end to end along the dimension named above; an argument that names none is the same for every part. Nothing has to cross between parts.
Inputs may be any that keep to these rules, and one draw needn't show every extreme that they name: `route`: each row names 2 different experts; within the 4 rows of one device no expert is named by more than 4 rows, and in some device's rows some expert is named by exactly 4 rows.
All inputs are finite; a program needn't handle non-finite values.
Results may differ from a plain program's by a relative error of at most 0.0066.
Values may be sent and summed in bfloat16 or wider, within the bound.
A program may use at most 128 MiB of HBM per device.

v0:
```python
import jax
import jax.numpy as jnp
from jax import lax
from jax.sharding import PartitionSpec as P


def dispatch_tables(route, gates, experts, capacity):
    tok_count, top_count = route.shape
    flat_route = route.reshape(-1)
    onehot = (flat_route[:, None] == jnp.arange(experts, dtype=jnp.int32)[None, :]).astype(
        jnp.int32
    )
    before = jnp.cumsum(onehot, axis=0) - onehot
    slot_index = jnp.sum(before * onehot, axis=1)
    target = (flat_route * capacity + slot_index).reshape(tok_count, top_count)
    columns = jnp.arange(experts * capacity, dtype=jnp.int32)
    matches = target[:, :, None] == columns[None, None, :]
    placement = jnp.any(matches, axis=1).T.astype(jnp.bfloat16)
    combine = jnp.sum(jnp.where(matches, gates[:, :, None], 0.0), axis=1)
    return (placement, combine)


def on_device(tokens, route, gates, w_gate, w_up, w_down):
    experts = lax.axis_size("ex")
    slices = lax.axis_size("ey")
    tok_count, features = tokens.shape
    top_count = route.shape[1]
    capacity = tok_count * top_count // experts + 2
    placement, combine = dispatch_tables(route, gates, experts, capacity)
    outgoing = jnp.dot(placement, tokens, preferred_element_type=jnp.float32).astype(jnp.bfloat16)
    outgoing = outgoing.reshape(experts, capacity, features)
    gate_cols = w_gate[0]
    up_cols = w_up[0]
    down_rows = w_down[0]
    copies = jnp.broadcast_to(outgoing[:, None], (experts, slices, capacity, features))
    copies = copies.reshape(experts * slices, capacity, features)
    arrived = lax.all_to_all(copies, ("ex", "ey"), split_axis=0, concat_axis=0, tiled=True).reshape(
        -1, features
    )
    pre_gate = jnp.dot(arrived, gate_cols, preferred_element_type=jnp.float32)
    pre_up = jnp.dot(arrived, up_cols, preferred_element_type=jnp.float32)
    hidden = (jax.nn.silu(pre_gate) * pre_up).astype(jnp.bfloat16)
    partial_value = jnp.dot(hidden, down_rows, preferred_element_type=jnp.float32).astype(
        jnp.bfloat16
    )
    partial_value = partial_value.reshape(experts * slices, capacity, features)
    returned = lax.all_to_all(partial_value, ("ex", "ey"), split_axis=0, concat_axis=0, tiled=True)
    summed = jnp.sum(
        returned.reshape(experts, slices, capacity, features).astype(jnp.float32), axis=1
    )
    results = summed.astype(jnp.bfloat16).reshape(experts * capacity, features)
    mixed = jnp.dot(combine, results.astype(jnp.float32), precision=lax.Precision.HIGHEST)
    return mixed.astype(jnp.bfloat16)


def solution(mesh):
    placed = (
        P(("groups", "ex", "ey"), None),
        P(("groups", "ex", "ey"), None),
        P(("groups", "ex", "ey"), None),
        P("ex", None, "ey"),
        P("ex", None, "ey"),
        P("ex", "ey", None),
    )
    return jax.shard_map(
        on_device,
        mesh=mesh,
        in_specs=placed,
        out_specs=P(("groups", "ex", "ey"), None),
        check_vma=False,
    )
```

profile of v0, /device:TPU:0, one launch (start us, length us, event | category | flops | bytes accessed | tf_op | source)
XLA Modules:
  0.0 72.2 jit_solution(8555893080562507745)
XLA Ops:
  0.0 0.0 copy-start
  0.0 0.8 %copy.13 = s32[4,2]{1,0:T(4,128)S(1)} copy(s32[4,2]{0,1:T(2,128)} %param.7) | data formatting | bytes 64 | tf_op args[1]
  0.8 0.1 eq.28
  0.9 0.2 reduce_window_sum.11
  1.1 0.1 reduce_sum.33
  1.2 0.1 copy.15
  1.3 0.1 fusion.19
  1.4 0.0 copy-done
  1.4 0.3 convolution_convert_fusion.1
  1.6 0.1 broadcast_in_dim.24
  1.7 0.2 broadcast_in_dim.25
  2.0 29.7 %all_to_all.10 = bf16[16,4,7168]{2,1,0:T(4,128)(2,1)S(1)} all-to-all(bf16[16,4,7168]{2,1,0:T(4,128)(2,1)S(1)} %bitcast.24), channel_id=1, replica_groups=mesh['groups'=2,'ex'=4,'ey'=4] {'ex','ey'}, dimensions={0} | all-to-all | bytes 1835008 | tf_op jit(solution)/shard_map/all_to_all | solution.py:37
  31.7 0.2 reshape.26
  31.9 4.5 %fusion.3 = f32[64,512]{1,0:T(8,128)S(1)} fusion(bf16[64,7168]{1,0:T(8,128)(2,1)S(1)} %reshape.26, bf16[1,7168,512]{2,1,0:T(8,128)(2,1)} %param.9), kind=kOutput, calls=%fused_computation.6 | convolution fusion | flops 469762048 | bytes 8388608 | tf_op jit(solution)/shard_map/dot_general | solution.py:40
  36.4 0.0 copy-start.1
  36.4 7.9 %convolution_convert_fusion = bf16[64,7168]{1,0:T(8,128)(2,1)S(1)} fusion(bf16[1,512,7168]{2,1,0:T(8,128)(2,1)} %param.11, bf16[64,7168]{1,0:T(8,128)(2,1)S(1)} %reshape.26, bf16[1,7168,512]{2,1,0:T(8,128)(2,1)} %param.10, f32[64,512]{1,0:T(8,128)S(1)} %fusion.3), kind=kOutput, calls=%fused_computation | convolution fusion | flops 940179456 | bytes 16646144 | tf_op jit(solution)/shard_map/dot_general | solution.py:43
  44.3 1.3 %reshape.27 = bf16[16,4,7168]{2,1,0:T(4,128)(2,1)} reshape(bf16[64,7168]{1,0:T(8,128)(2,1)S(1)} %convolution_convert_fusion) | data formatting | bytes 1835008 | tf_op jit(solution)/shard_map/reshape | solution.py:46
  45.6 4.5 %all-to-all-start.1 = ((bf16[16,4,7168]{2,1,0:T(4,128)(2,1)}), bf16[16,4,7168]{2,1,0:T(4,128)(2,1)S(1)}, u32[]{:S(2)}, u32[]{:S(2)}) async-start(bf16[16,4,7168]{2,1,0:T(4,128)(2,1)} %reshape.27), calls=%async_computation.1 | async-start | bytes 1835008 | tf_op jit(solution)/shard_map/all_to_all | solution.py:47
  50.0 0.0 copy-done.1
  50.0 0.1 select_reduce_fusion
  50.1 20.7 %all-to-all-done.1 = bf16[16,4,7168]{2,1,0:T(4,128)(2,1)S(1)} async-done(((bf16[16,4,7168]{2,1,0:T(4,128)(2,1)}), bf16[16,4,7168]{2,1,0:T(4,128)(2,1)S(1)}, u32[]{:S(2)}, u32[]{:S(2)}) %all-to-all-start.1) | async-done | bytes 917536 | tf_op jit(solution)/shard_map/all_to_all | solution.py:47
  70.9 0.5 bitcast_reduce_fusion
  71.3 0.1 reshape.29
  71.4 0.9 %convolution_convert_fusion.2 = bf16[4,7168]{1,0:T(4,128)(2,1)} fusion(f32[4,16]{1,0:T(4,128)S(1)} %select_reduce_fusion, bf16[16,7168]{1,0:T(8,128)(2,1)S(1)} %reshape.29), kind=kOutput, calls=%fused_computation.2 | convolution fusion | flops 5533696 | bytes 286976 | tf_op jit(solution)/shard_map/dot_general | solution.py:52
  (3 shorter events, 0.0 us)
Async XLA Ops:
  0.0 1.4 %copy-start = (bf16[4,7168]{1,0:T(4,128)(2,1)S(1)}, bf16[4,7168]{1,0:T(4,128)(2,1)}, u32[]{:S(2)}) copy-start(bf16[4,7168]{1,0:T(4,128)(2,1)} %param.6) | copy-start | bytes 172036
  36.4 13.7 %copy-start.1 = (f32[4,2]{0,1:T(2,128)S(1)}, f32[4,2]{0,1:T(2,128)}, u32[]{:S(2)}) copy-start(f32[4,2]{0,1:T(2,128)} %param.8) | copy-start | bytes 100
  45.6 25.3 %all-to-all-start.1 = ((bf16[16,4,7168]{2,1,0:T(4,128)(2,1)}), bf16[16,4,7168]{2,1,0:T(4,128)(2,1)S(1)}, u32[]{:S(2)}, u32[]{:S(2)}) async-start(bf16[16,4,7168]{2,1,0:T(4,128)(2,1)} %reshape.27), calls=%async_computation.1 | async-start | bytes 1835008 | tf_op jit(solution)/shard_map/all_to_all | solution.py:47
where the time goes:
time: 73.1 us; the launch traced here: 72.2 us
  blocking collectives  29.7 us (41%)
  waiting for transfers between devices  20.7 us (28%)
  matrix products  13.5 us (18%)
  starting transfers between devices  4.48 us (6%)
  local copies, waits for them, and re-layouts  2.91 us (4%)
  other arithmetic  0.84 us (1%)
    all_to_all x1, blocking collectives, on_device(): lax.all_to_all(copies, ('ex', 'ey'), split_axis=0, concat_axis=0, tiled=T...  29.7 us
    all_to_all x1, waiting for transfers between devices, on_device(): lax.all_to_all(partial_value, ('ex', 'ey'), split_axis=0, concat_axis=0,...  20.7 us
    dot_general x1, matrix products, on_device(): jnp.dot(hidden, down_rows, preferred_element_type=jnp.float32)  7.91 us
    all_to_all x1, starting transfers between devices, on_device(): lax.all_to_all(partial_value, ('ex', 'ey'), split_axis=0, concat_axis=0,...  4.48 us
    dot_general x1, matrix products, on_device(): pre_gate = jnp.dot(arrived, gate_cols, preferred_element_type=jnp.float32)  4.45 us
  transfers between devices with their start and end apart: 1, of which 1 were waited for; matrix products, arithmetic and copies ran while one was open for 0% of the time, Pallas kernels for 0%

commit v1 on v0

v1 whole, which is shorter than its diff:
```python
import functools

import jax
import jax.numpy as jnp
from jax import lax
from jax.experimental import pallas as pl
from jax.experimental.pallas import tpu as pltpu
from jax.sharding import PartitionSpec as P

F32 = jnp.float32
BF16 = jnp.bfloat16
ROWS = 16


def pick(shape, toks, inverse):
    n = shape[0]
    devs = n // ROWS
    q_of = ROWS // toks
    r = lax.broadcasted_iota(jnp.int32, shape, 1 if inverse else 0)
    k = lax.broadcasted_iota(jnp.int32, shape, 0 if inverse else 1)
    per_q = devs * toks
    q, rest = r // per_q, r % per_q
    want = (rest // toks) * (q_of * toks) + q * toks + rest % toks
    return jnp.where(want == k, 1.0, 0.0).astype(BF16)


def kernel(cfg, tok_ref, route_ref, gate_ref, wg_hbm, wu_hbm, wd_hbm, out_ref,
           wg, wu, wd, x, xa, acc_g, acc_u, y, r_sib, s1, r_x, s2, r_z,
           w_sem, ag_zs, ag_zr, ag_xs, ag_xr, ag_ss, ag_sr,
           rs_zs, rs_zr, rs_xs, rs_xr, rs_ss, rs_sr):
    nz, nx, chunks, w, toks, quarters = cfg
    ndev = 2 * nx * nz
    grp = min(ndev, 16)
    ngrp = ndev // grp
    quarter = chunks * w
    hid = wg.shape[2]
    z = lax.axis_index("ex")
    ey = lax.axis_index("ey")
    xi = ey // 2
    core = ey % 2

    def dev(zz, xx, cc):
        return {"ex": zz, "ey": xx * 2 + cc}

    def load_w(j):
        rows = pl.ds(j * w, w)
        return [pltpu.make_async_copy(wg_hbm.at[:, rows, :], wg.at[:, rows, :], w_sem.at[0, j]),
                pltpu.make_async_copy(wu_hbm.at[:, rows, :], wu.at[:, rows, :], w_sem.at[1, j])]

    def load_d(q):
        cols = pl.ds(q * quarter, quarter)
        return pltpu.make_async_copy(wd_hbm.at[:, cols], wd.at[:, cols], w_sem.at[2, q])

    for j in range(chunks):
        for c in load_w(j):
            c.start()
    for q in range(quarters):
        load_d(q).start()

    barrier = pltpu.get_barrier_semaphore()
    zs = [lax.rem(z + i, nz) for i in range(1, nz)]
    xs = [lax.rem(xi + i, nx) for i in range(1, nx)]
    for zz in zs:
        pl.semaphore_signal(barrier, inc=1, device_id=dev(zz, xi, core), device_id_type=pl.DeviceIdType.MESH)
    for xx in xs:
        pl.semaphore_signal(barrier, inc=1, device_id=dev(z, xx, core), device_id_type=pl.DeviceIdType.MESH)
    pl.semaphore_signal(barrier, inc=1, device_id=dev(z, xi, 1 - core), device_id_type=pl.DeviceIdType.MESH)

    t = tok_ref[...].astype(F32)
    for j in range(chunks):
        parts = [t[:, q * quarter + j * w:q * quarter + (j + 1) * w] for q in range(quarters)]
        x[j, core, xi, z] = jnp.concatenate(parts, axis=0).astype(BF16)
    rt = route_ref[...].astype(F32)
    gt = gate_ref[...]
    eye = lax.broadcasted_iota(jnp.int32, (toks, toks), 0) == lax.broadcasted_iota(jnp.int32, (toks, toks), 1)
    lane = lax.broadcasted_iota(jnp.int32, (toks, 128), 1).astype(F32)
    a = jnp.zeros((toks, 128), F32)
    for k in range(rt.shape[0]):
        rc = jnp.sum(jnp.where(eye, jnp.broadcast_to(rt[k:k + 1, :], (toks, toks)), 0.0), axis=1, keepdims=True)
        gc = jnp.sum(jnp.where(eye, jnp.broadcast_to(gt[k:k + 1, :], (toks, toks)), 0.0), axis=1, keepdims=True)
        a = a + jnp.where(lane == rc, gc, 0.0)
    hi = a.astype(BF16).astype(F32)
    mid = (a - hi).astype(BF16).astype(F32)
    low = a - hi - mid
    terms = [hi, mid, low] + [jnp.zeros_like(a)] * (quarters - 3)
    xa[core, xi, z] = jnp.concatenate(terms, axis=0).astype(BF16)

    pl.semaphore_wait(barrier, (nz - 1) + (nx - 1) + 1)

    def buf(j):
        return x.at[j] if j < chunks else xa

    def remote(src, dst, ss, rs, to):
        return pltpu.make_async_remote_copy(src_ref=src, dst_ref=dst, send_sem=ss, recv_sem=rs,
                                            device_id=to, device_id_type=pl.DeviceIdType.MESH)

    def ag_z(j, i, incoming=False):
        at = lax.rem(z + nz - i, nz) if incoming else z
        b = buf(j).at[core, xi, at]
        return remote(b, b, ag_zs.at[j, i], ag_zr.at[j, i], dev(lax.rem(z + i, nz), xi, core))

    def ag_x(j, i, incoming=False):
        at = lax.rem(xi + nx - i, nx) if incoming else xi
        b = buf(j).at[core, at]
        return remote(b, b, ag_xs.at[j, i], ag_xr.at[j, i], dev(z, lax.rem(xi + i, nx), core))

    def ag_s(j, incoming=False):
        b = buf(j).at[1 - core if incoming else core]
        return remote(b, b, ag_ss.at[j], ag_sr.at[j], dev(z, xi, 1 - core))

    order = list(range(chunks)) + [chunks]
    for j in order:
        for i in range(1, nz):
            ag_z(j, i).start()

    fwd = pick((grp * ROWS, grp * ROWS), toks, False)
    per_q = grp * toks

    def arrange(ref, width):
        whole = ref[...].reshape(ndev * ROWS, width)
        got = []
        for g in range(ngrp):
            got.append(jnp.dot(fwd, whole[g * grp * ROWS:(g + 1) * grp * ROWS], preferred_element_type=F32))
        return [jnp.concatenate([p[q * per_q:(q + 1) * per_q] for p in got], axis=0) for q in range(quarters)]

    def gate_up(j):
        for c in load_w(j):
            c.wait()
        rows = pl.ds(j * w, w)
        xc = jnp.concatenate([p.astype(BF16) for p in arrange(x.at[j], w)], axis=1)
        for acc, wt in ((acc_g, wg), (acc_u, wu)):
            d = jnp.dot(xc, wt[:, rows, :].reshape(quarters * w, hid), preferred_element_type=F32)
            acc[...] = d if j == 0 else acc[...] + d

    total = chunks + 1
    for i in range(total + 2):
        if i < total:
            for k in range(1, nz):
                ag_z(i, k, True).wait_recv()
            for k in range(1, nx):
                ag_x(i, k).start()
        if 0 <= i - 1 < total:
            for k in range(1, nx):
                ag_x(i - 1, k, True).wait_recv()
            ag_s(i - 1).start()
        if 0 <= i - 2 < total:
            ag_s(i - 2, True).wait_recv()
            if i - 2 < chunks:
                gate_up(i - 2)

    own = lax.broadcasted_iota(jnp.int32, (ndev * toks, 128), 1) == z
    aa = functools.reduce(lambda p, q: p + q, arrange(xa, 128)[:3])
    share = jnp.sum(jnp.where(own, aa, 0.0), axis=1, keepdims=True)
    g = acc_g[...]
    h = (g / (1.0 + jnp.exp(-g)) * acc_u[...]).astype(BF16)
    back = pick((grp * ROWS, grp * ROWS), toks, True)

    def rs_s(j):
        return remote(y.at[j, 1 - core], r_sib.at[j], rs_ss.at[j], rs_sr.at[j], dev(z, xi, 1 - core))

    def rs_x(j, i):
        return remote(s1.at[j, lax.rem(xi + i, nx)], r_x.at[j, i], rs_xs.at[j, i], rs_xr.at[j, i],
                      dev(z, lax.rem(xi + i, nx), core))

    def rs_z(j, i):
        return remote(s2.at[j, lax.rem(z + i, nz)], r_z.at[j, i], rs_zs.at[j, i], rs_zr.at[j, i],
                      dev(lax.rem(z + i, nz), xi, core))

    for q in range(quarters):
        load_d(q).wait()

    def down(j):
        terms = []
        for q in range(quarters):
            d = jnp.dot(h, wd[:, q * quarter + j * w:q * quarter + (j + 1) * w], preferred_element_type=F32)
            terms.append((d * share).astype(BF16))
        out = []
        for gi in range(ngrp):
            rows = jnp.concatenate([v[gi * per_q:(gi + 1) * per_q] for v in terms], axis=0)
            out.append(jnp.dot(back, rows, preferred_element_type=F32).astype(BF16))
        y[j] = jnp.concatenate(out, axis=0).reshape(2, nx, nz, ROWS, w)
        rs_s(j).start()

    def stage_x(j):
        rs_s(j).wait_recv()
        s1[j] = (y[j, core].astype(F32) + r_sib[j].astype(F32)).astype(BF16)
        for i in range(1, nx):
            rs_x(j, i).start()

    def stage_z(j):
        v = s1[j, xi].astype(F32)
        for i in range(1, nx):
            rs_x(j, i).wait_recv()
            v = v + r_x[j, i].astype(F32)
        s2[j] = v.astype(BF16)
        for i in range(1, nz):
            rs_z(j, i).start()

    def stage_out(j):
        v = s2[j, z].astype(F32)
        for i in range(1, nz):
            rs_z(j, i).wait_recv()
            v = v + r_z[j, i].astype(F32)
        for q in range(quarters):
            out_ref[:, q * quarter + j * w:q * quarter + (j + 1) * w] = v[q * toks:(q + 1) * toks].astype(BF16)

    stages = ((down, 0), (stage_x, 1), (stage_z, 2), (stage_out, 4))
    for i in range(chunks + 4):
        for fn, lag in stages:
            if 0 <= i - lag < chunks:
                fn(i - lag)

    for j in order:
        for i in range(1, nz):
            ag_z(j, i).wait_send()
        for i in range(1, nx):
            ag_x(j, i).wait_send()
        ag_s(j).wait_send()
    for j in range(chunks):
        for i in range(1, nz):
            rs_z(j, i).wait_send()
        for i in range(1, nx):
            rs_x(j, i).wait_send()
        rs_s(j).wait_send()


def chunk_count(quarter):
    lanes = quarter // 128
    return lanes // 2 if lanes % 2 == 0 else lanes


def on_device(tokens, route, gates, w_gate, w_up, w_down):
    nz = lax.axis_size("ex")
    nx = lax.axis_size("ey") // 2
    toks, width = tokens.shape
    quarters = ROWS // toks
    quarter = width // quarters
    hid = w_gate.shape[2]
    chunks = chunk_count(quarter)
    w = quarter // chunks
    ndev = 2 * nx * nz
    cfg = (nz, nx, chunks, w, toks, quarters)
    dma = pltpu.SemaphoreType.DMA
    vm = pl.BlockSpec(memory_space=pltpu.VMEM)
    hbm = pl.BlockSpec(memory_space=pl.ANY)
    return pl.pallas_call(
        functools.partial(kernel, cfg),
        out_shape=jax.ShapeDtypeStruct((toks, width), BF16),
        in_specs=[vm, vm, vm, hbm, hbm, hbm],
        out_specs=vm,
        scratch_shapes=[
            pltpu.VMEM((quarters, quarter, hid), BF16),
            pltpu.VMEM((quarters, quarter, hid), BF16),
            pltpu.VMEM((hid, width), BF16),
            pltpu.VMEM((chunks, 2, nx, nz, ROWS, w), BF16),
            pltpu.VMEM((2, nx, nz, ROWS, 128), BF16),
            pltpu.VMEM((ndev * toks, hid), F32),
            pltpu.VMEM((ndev * toks, hid), F32),
            pltpu.VMEM((chunks, 2, nx, nz, ROWS, w), BF16),
            pltpu.VMEM((chunks, nx, nz, ROWS, w), BF16),
            pltpu.VMEM((chunks, nx, nz, ROWS, w), BF16),
            pltpu.VMEM((chunks, nx, nz, ROWS, w), BF16),
            pltpu.VMEM((chunks, nz, ROWS, w), BF16),
            pltpu.VMEM((chunks, nz, ROWS, w), BF16),
            dma((3, max(chunks, quarters))),
            dma((chunks + 1, nz)), dma((chunks + 1, nz)),
            dma((chunks + 1, nx)), dma((chunks + 1, nx)),
            dma((chunks + 1,)), dma((chunks + 1,)),
            dma((chunks, nz)), dma((chunks, nz)),
            dma((chunks, nx)), dma((chunks, nx)),
            dma((chunks,)), dma((chunks,)),
        ],
        compiler_params=pltpu.CompilerParams(
            collective_id=0, has_side_effects=True, vmem_limit_bytes=56 * 1024 * 1024
        ),
    )(tokens, route.T, gates.T, w_gate.reshape(quarters, quarter, hid),
      w_up.reshape(quarters, quarter, hid), w_down[0])


def solution(mesh):
    placed = (
        P(("groups", "ex", "ey"), None),
        P(("groups", "ex", "ey"), None),
        P(("groups", "ex", "ey"), None),
        P("ex", None, "ey"),
        P("ex", None, "ey"),
        P("ex", "ey", None),
    )
    return jax.shard_map(
        on_device,
        mesh=mesh,
        in_specs=placed,
        out_specs=P(("groups", "ex", "ey"), None),
        check_vma=False,
    )
```

time: 73.1 us -> 47.2 us (0.65)
  Pallas kernels: 0 us -> 45.5 us
  blocking collectives: 29.7 us -> 0 us
  waiting for transfers between devices: 20.7 us -> 0 us
  matrix products: 13.5 us -> 0 us
  starting transfers between devices: 4.48 us -> 0 us
  local copies, waits for them, and re-layouts: 2.91 us -> 1.46 us
  other arithmetic: 0.84 us -> 0 us
    pallas_call x0 -> x1, Pallas kernels: none -> 45.5 us  [on_device(): pl.pallas_call(functools.partial(kernel, cfg), out_shape=jax.ShapeDtypeSt...]
    all_to_all x1 -> x0, blocking collectives: 29.7 us -> none  [on_device(): lax.all_to_all(copies, ('ex', 'ey'), split_axis=0, concat_axis=0, tiled=T...]
    all_to_all x1 -> x0, waiting for transfers between devices: 20.7 us -> none  [on_device(): lax.all_to_all(partial_value, ('ex', 'ey'), split_axis=0, concat_axis=0,...]
    dot_general x4 -> x0, matrix products: 13.5 us -> none  [the longest x1 7.91 us: on_device(): jnp.dot(hidden, down_rows, preferred_element_type=jnp.float32)]
    all_to_all x1 -> x0, starting transfers between devices: 4.48 us -> none  [on_device(): lax.all_to_all(partial_value, ('ex', 'ey'), split_axis=0, concat_axis=0,...]
    reshape x3 -> x0, local copies, waits for them, and re-layouts: 1.52 us -> none  [the longest x1 1.26 us: on_device(): partial_value = partial_value.reshape(experts * slices, capacity, features)]
    unnamed x5 -> x1, local copies, waits for them, and re-layouts: 0.78 us -> 1.46 us
  transfers between devices with their start and end apart: 1 -> 0, of which waited for: 1 -> 0; matrix products, arithmetic and copies ran while one was open for 0% -> 0% of each run, Pallas kernels for 0% -> 0%
where the time goes in v1:
time: 47.2 us; the launch traced here: 47 us
  Pallas kernels  45.5 us (96%)
  local copies, waits for them, and re-layouts  1.46 us (3%)
    pallas_call x1, Pallas kernels, on_device(): pl.pallas_call(functools.partial(kernel, cfg), out_shape=jax.ShapeDtypeSt...  45.5 us
    unnamed x1, local copies, waits for them, and re-layouts  1.46 us

profile of v1, /device:TPU:0, one launch (start us, length us, event | category | flops | bytes accessed | tf_op | source)
XLA Modules:
  0.0 47.0 jit_solution(3931875776759594095)
XLA Ops:
  0.0 45.5 %shard_map.64 = bf16[4,7168]{1,0:T(4,128)(2,1)} custom-call(bf16[4,7168]{1,0:T(4,128)(2,1)} %tok_ref.1, s32[2,4]{1,0:T(2,128)} %bitcast.8, f32[2,4]{1,0:T(2,128)} %bitcast.9, bf16[4,1792,512]{2,1,0:T(8,128)(2,1)} %bitcast.5, bf16[4,1792,512]{2,1,0:T(8,128)(2,1)} %bitcast.6, bf16[512,7168]{1,0:T(8,128)(2,1)} %bitcast.7), custom_call_target="tpu_custom_call" | custom-call | tf_op jit(solution)/shard_map/pallas_call | solution.py:246
  45.6 1.5 %copy.8 = bf16[4,7168]{1,0:T(4,128)(2,1)} copy(bf16[4,7168]{1,0:T(4,128)(2,1)} %shard_map.64) | data formatting | bytes 114688

commit v2 on v1

--- a/solution.py
+++ b/solution.py
@@ -28,22 +28,27 @@
            wg, wu, wd, x, xa, acc_g, acc_u, y, r_sib, s1, r_x, s2, r_z,
            w_sem, ag_zs, ag_zr, ag_xs, ag_xr, ag_ss, ag_sr,
            rs_zs, rs_zr, rs_xs, rs_xr, rs_ss, rs_sr):
-    nz, nx, chunks, w, toks, quarters = cfg
+    nz, nx, widths, toks, quarters = cfg
     ndev = 2 * nx * nz
     grp = min(ndev, 16)
     ngrp = ndev // grp
-    quarter = chunks * w
+    chunks = len(widths)
+    quarter = sum(widths)
+    starts = [sum(widths[:j]) for j in range(chunks)]
     hid = wg.shape[2]
     z = lax.axis_index("ex")
     ey = lax.axis_index("ey")
     xi = ey // 2
     core = ey % 2
 
+    def lanes(q, j):
+        return slice(q * quarter + starts[j], q * quarter + starts[j] + widths[j])
+
     def dev(zz, xx, cc):
         return {"ex": zz, "ey": xx * 2 + cc}
 
     def load_w(j):
-        rows = pl.ds(j * w, w)
+        rows = pl.ds(starts[j], widths[j])
         return [pltpu.make_async_copy(wg_hbm.at[:, rows, :], wg.at[:, rows, :], w_sem.at[0, j]),
                 pltpu.make_async_copy(wu_hbm.at[:, rows, :], wu.at[:, rows, :], w_sem.at[1, j])]
 
@@ -68,8 +73,8 @@
 
     t = tok_ref[...].astype(F32)
     for j in range(chunks):
-        parts = [t[:, q * quarter + j * w:q * quarter + (j + 1) * w] for q in range(quarters)]
-        x[j, core, xi, z] = jnp.concatenate(parts, axis=0).astype(BF16)
+        parts = [t[:, lanes(q, j)] for q in range(quarters)]
+        x[j][core, xi, z] = jnp.concatenate(parts, axis=0).astype(BF16)
     rt = route_ref[...].astype(F32)
     gt = gate_ref[...]
     eye = lax.broadcasted_iota(jnp.int32, (toks, toks), 0) == lax.broadcasted_iota(jnp.int32, (toks, toks), 1)
@@ -88,30 +93,37 @@
     pl.semaphore_wait(barrier, (nz - 1) + (nx - 1) + 1)
 
     def buf(j):
-        return x.at[j] if j < chunks else xa
+        return x[j] if j < chunks else xa
 
     def remote(src, dst, ss, rs, to):
         return pltpu.make_async_remote_copy(src_ref=src, dst_ref=dst, send_sem=ss, recv_sem=rs,
                                             device_id=to, device_id_type=pl.DeviceIdType.MESH)
 
+    last = chunks - 1
+
     def ag_z(j, i, incoming=False):
         at = lax.rem(z + nz - i, nz) if incoming else z
-        b = buf(j).at[core, xi, at]
+        b = buf(j).at[core, :, at] if j == last else buf(j).at[core, xi, at]
         return remote(b, b, ag_zs.at[j, i], ag_zr.at[j, i], dev(lax.rem(z + i, nz), xi, core))
 
     def ag_x(j, i, incoming=False):
         at = lax.rem(xi + nx - i, nx) if incoming else xi
-        b = buf(j).at[core, at]
+        b = buf(j).at[core, at, z] if j == last else buf(j).at[core, at]
         return remote(b, b, ag_xs.at[j, i], ag_xr.at[j, i], dev(z, lax.rem(xi + i, nx), core))
 
     def ag_s(j, incoming=False):
         b = buf(j).at[1 - core if incoming else core]
         return remote(b, b, ag_ss.at[j], ag_sr.at[j], dev(z, xi, 1 - core))
 
+    def hops(first, j):
+        along_z = first != (j == last)
+        return (ag_z, nz) if along_z else (ag_x, nx)
+
     order = list(range(chunks)) + [chunks]
     for j in order:
-        for i in range(1, nz):
-            ag_z(j, i).start()
+        fn, n = hops(True, j)
+        for i in range(1, n):
+            fn(j, i).start()
 
     fwd = pick((grp * ROWS, grp * ROWS), toks, False)
     per_q = grp * toks
@@ -126,27 +138,28 @@
     def gate_up(j):
         for c in load_w(j):
             c.wait()
-        rows = pl.ds(j * w, w)
-        xc = jnp.concatenate([p.astype(BF16) for p in arrange(x.at[j], w)], axis=1)
+        rows = pl.ds(starts[j], widths[j])
+        xc = jnp.concatenate([p.astype(BF16) for p in arrange(x[j], widths[j])], axis=1)
         for acc, wt in ((acc_g, wg), (acc_u, wu)):
-            d = jnp.dot(xc, wt[:, rows, :].reshape(quarters * w, hid), preferred_element_type=F32)
+            d = jnp.dot(xc, wt[:, rows, :].reshape(quarters * widths[j], hid), preferred_element_type=F32)
             acc[...] = d if j == 0 else acc[...] + d
 
-    total = chunks + 1
-    for i in range(total + 2):
-        if i < total:
-            for k in range(1, nz):
-                ag_z(i, k, True).wait_recv()
-            for k in range(1, nx):
-                ag_x(i, k).start()
-        if 0 <= i - 1 < total:
-            for k in range(1, nx):
-                ag_x(i - 1, k, True).wait_recv()
-            ag_s(i - 1).start()
-        if 0 <= i - 2 < total:
-            ag_s(i - 2, True).wait_recv()
-            if i - 2 < chunks:
-                gate_up(i - 2)
+    for j in [last] + [j for j in order if j != last]:
+        fn, n = hops(True, j)
+        for i in range(1, n):
+            fn(j, i, True).wait_recv()
+        fn, n = hops(False, j)
+        for i in range(1, n):
+            fn(j, i).start()
+    for j in order:
+        fn, n = hops(False, j)
+        for i in range(1, n):
+            fn(j, i, True).wait_recv()
+        ag_s(j).start()
+    for j in order:
+        ag_s(j, True).wait_recv()
+        if j < chunks:
+            gate_up(j)
 
     own = lax.broadcasted_iota(jnp.int32, (ndev * toks, 128), 1) == z
     aa = functools.reduce(lambda p, q: p + q, arrange(xa, 128)[:3])
@@ -156,15 +169,17 @@
     back = pick((grp * ROWS, grp * ROWS), toks, True)
 
     def rs_s(j):
-        return remote(y.at[j, 1 - core], r_sib.at[j], rs_ss.at[j], rs_sr.at[j], dev(z, xi, 1 - core))
+        return remote(y[j].at[1 - core], r_sib[j], rs_ss.at[j], rs_sr.at[j], dev(z, xi, 1 - core))
 
     def rs_x(j, i):
-        return remote(s1.at[j, lax.rem(xi + i, nx)], r_x.at[j, i], rs_xs.at[j, i], rs_xr.at[j, i],
-                      dev(z, lax.rem(xi + i, nx), core))
+        to = lax.rem(xi + i, nx)
+        src = s2[j].at[to] if j == last else s1[j].at[to]
+        return remote(src, r_x[j].at[i], rs_xs.at[j, i], rs_xr.at[j, i], dev(z, to, core))
 
     def rs_z(j, i):
-        return remote(s2.at[j, lax.rem(z + i, nz)], r_z.at[j, i], rs_zs.at[j, i], rs_zr.at[j, i],
-                      dev(lax.rem(z + i, nz), xi, core))
+        to = lax.rem(z + i, nz)
+        src = s1[j].at[:, to] if j == last else s2[j].at[to]
+        return remote(src, r_z[j].at[i], rs_zs.at[j, i], rs_zr.at[j, i], dev(to, xi, core))
 
     for q in range(quarters):
         load_d(q).wait()
@@ -172,43 +187,59 @@
     def down(j):
         terms = []
         for q in range(quarters):
-            d = jnp.dot(h, wd[:, q * quarter + j * w:q * quarter + (j + 1) * w], preferred_element_type=F32)
+            d = jnp.dot(h, wd[:, lanes(q, j)], preferred_element_type=F32)
             terms.append((d * share).astype(BF16))
         out = []
         for gi in range(ngrp):
             rows = jnp.concatenate([v[gi * per_q:(gi + 1) * per_q] for v in terms], axis=0)
             out.append(jnp.dot(back, rows, preferred_element_type=F32).astype(BF16))
-        y[j] = jnp.concatenate(out, axis=0).reshape(2, nx, nz, ROWS, w)
+        y[j][...] = jnp.concatenate(out, axis=0).reshape(2, nx, nz, ROWS, widths[j])
         rs_s(j).start()
 
-    def stage_x(j):
+    def first_hop(j):
         rs_s(j).wait_recv()
-        s1[j] = (y[j, core].astype(F32) + r_sib[j].astype(F32)).astype(BF16)
-        for i in range(1, nx):
-            rs_x(j, i).start()
-
-    def stage_z(j):
-        v = s1[j, xi].astype(F32)
-        for i in range(1, nx):
-            rs_x(j, i).wait_recv()
-            v = v + r_x[j, i].astype(F32)
-        s2[j] = v.astype(BF16)
-        for i in range(1, nz):
-            rs_z(j, i).start()
+        s1[j][...] = (y[j][core].astype(F32) + r_sib[j][...].astype(F32)).astype(BF16)
+        fn, n = (rs_z, nz) if j == last else (rs_x, nx)
+        for i in range(1, n):
+            fn(j, i).start()
+
+    def second_hop(j):
+        if j == last:
+            v = s1[j][:, z].astype(F32)
+            for i in range(1, nz):
+                rs_z(j, i).wait_recv()
+                v = v + r_z[j][i].astype(F32)
+        else:
+            v = s1[j][xi].astype(F32)
+            for i in range(1, nx):
+                rs_x(j, i).wait_recv()
+                v = v + r_x[j][i].astype(F32)
+        s2[j][...] = v.astype(BF16)
+        fn, n = (rs_x, nx) if j == last else (rs_z, nz)
+        for i in range(1, n):
+            fn(j, i).start()
 
     def stage_out(j):
-        v = s2[j, z].astype(F32)
-        for i in range(1, nz):
-            rs_z(j, i).wait_recv()
-            v = v + r_z[j, i].astype(F32)
+        if j == last:
+            v = s2[j][xi].astype(F32)
+            for i in range(1, nx):
+                rs_x(j, i).wait_recv()
+                v = v + r_x[j][i].astype(F32)
+        else:
+            v = s2[j][z].astype(F32)
+            for i in range(1, nz):
+                rs_z(j, i).wait_recv()
+                v = v + r_z[j][i].astype(F32)
         for q in range(quarters):
-            out_ref[:, q * quarter + j * w:q * quarter + (j + 1) * w] = v[q * toks:(q + 1) * toks].astype(BF16)
-
-    stages = ((down, 0), (stage_x, 1), (stage_z, 2), (stage_out, 4))
-    for i in range(chunks + 4):
-        for fn, lag in stages:
-            if 0 <= i - lag < chunks:
-                fn(i - lag)
+            out_ref[:, lanes(q, j)] = v[q * toks:(q + 1) * toks].astype(BF16)
+
+    turns = [last] + list(range(last))
+    for fn in (down, first_hop):
+        for j in turns:
+            fn(j)
+    for fn in (second_hop, stage_out):
+        for j in turns[::-1] if fn is second_hop else turns:
+            fn(j)
 
     for j in order:
         for i in range(1, nz):
@@ -224,9 +255,10 @@
         rs_s(j).wait_send()
 
 
-def chunk_count(quarter):
-    lanes = quarter // 128
-    return lanes // 2 if lanes % 2 == 0 else lanes
+def chunk_widths(quarter):
+    n = quarter // 128
+    small = max(1, (n * 6) // 14)
+    return ((n - small) * 128, small * 128)
 
 
 def on_device(tokens, route, gates, w_gate, w_up, w_down):
@@ -236,11 +268,16 @@
     quarters = ROWS // toks
     quarter = width // quarters
     hid = w_gate.shape[2]
-    chunks = chunk_count(quarter)
-    w = quarter // chunks
+    widths = chunk_widths(quarter)
+    chunks = len(widths)
+    last = chunks - 1
     ndev = 2 * nx * nz
-    cfg = (nz, nx, chunks, w, toks, quarters)
+    cfg = (nz, nx, widths, toks, quarters)
     dma = pltpu.SemaphoreType.DMA
+
+    def per_chunk(lead):
+        return [pltpu.VMEM(lead(j) + (ROWS, widths[j]), BF16) for j in range(chunks)]
+
     vm = pl.BlockSpec(memory_space=pltpu.VMEM)
     hbm = pl.BlockSpec(memory_space=pl.ANY)
     return pl.pallas_call(
@@ -252,16 +289,16 @@
             pltpu.VMEM((quarters, quarter, hid), BF16),
             pltpu.VMEM((quarters, quarter, hid), BF16),
             pltpu.VMEM((hid, width), BF16),
-            pltpu.VMEM((chunks, 2, nx, nz, ROWS, w), BF16),
+            per_chunk(lambda j: (2, nx, nz)),
             pltpu.VMEM((2, nx, nz, ROWS, 128), BF16),
             pltpu.VMEM((ndev * toks, hid), F32),
             pltpu.VMEM((ndev * toks, hid), F32),
-            pltpu.VMEM((chunks, 2, nx, nz, ROWS, w), BF16),
-            pltpu.VMEM((chunks, nx, nz, ROWS, w), BF16),
-            pltpu.VMEM((chunks, nx, nz, ROWS, w), BF16),
-            pltpu.VMEM((chunks, nx, nz, ROWS, w), BF16),
-            pltpu.VMEM((chunks, nz, ROWS, w), BF16),
-            pltpu.VMEM((chunks, nz, ROWS, w), BF16),
+            per_chunk(lambda j: (2, nx, nz)),
+            per_chunk(lambda j: (nx, nz)),
+            per_chunk(lambda j: (nx, nz)),
+            per_chunk(lambda j: (nx,) if j == last else (nx, nz)),
+            per_chunk(lambda j: (nx,) if j == last else (nz,)),
+            per_chunk(lambda j: (nz, nx) if j == last else (nz,)),
             dma((3, max(chunks, quarters))),
             dma((chunks + 1, nz)), dma((chunks + 1, nz)),
             dma((chunks + 1, nx)), dma((chunks + 1, nx)),

time: 47.2 us -> 33.6 us (0.71)
  Pallas kernels: 45.5 us -> 31.9 us
    pallas_call x1, Pallas kernels: 45.5 us -> 31.9 us  [on_device(): pl.pallas_call(functools.partial(kernel, cfg), out_shape=jax.ShapeDtypeSt...]
where the time goes in v2:
time: 33.6 us; the launch traced here: 33.4 us
  Pallas kernels  31.9 us (95%)
  local copies, waits for them, and re-layouts  1.46 us (4%)
    pallas_call x1, Pallas kernels, on_device(): pl.pallas_call(functools.partial(kernel, cfg), out_shape=jax.ShapeDtypeSt...  31.9 us
    unnamed x1, local copies, waits for them, and re-layouts  1.46 us

profile of v2, /device:TPU:0, one launch (start us, length us, event | category | flops | bytes accessed | tf_op | source)
XLA Modules:
  0.0 33.4 jit_solution(2795693485501861391)
XLA Ops:
  0.0 31.9 %shard_map.64 = bf16[4,7168]{1,0:T(4,128)(2,1)} custom-call(bf16[4,7168]{1,0:T(4,128)(2,1)} %tok_ref.1, s32[2,4]{1,0:T(2,128)} %bitcast.8, f32[2,4]{1,0:T(2,128)} %bitcast.9, bf16[4,1792,512]{2,1,0:T(8,128)(2,1)} %bitcast.5, bf16[4,1792,512]{2,1,0:T(8,128)(2,1)} %bitcast.6, bf16[512,7168]{1,0:T(8,128)(2,1)} %bitcast.7), custom_call_target="tpu_custom_call" | custom-call | tf_op jit(solution)/shard_map/pallas_call | solution.py:283
  31.9 1.5 %copy.8 = bf16[4,7168]{1,0:T(4,128)(2,1)} copy(bf16[4,7168]{1,0:T(4,128)(2,1)} %shard_map.64) | data formatting | bytes 114688

commit v3 on v2

--- a/solution.py
+++ b/solution.py
@@ -25,7 +25,7 @@
 
 
 def kernel(cfg, tok_ref, route_ref, gate_ref, wg_hbm, wu_hbm, wd_hbm, out_ref,
-           wg, wu, wd, x, xa, acc_g, acc_u, y, r_sib, s1, r_x, s2, r_z,
+           wg, wu, wd, x, acc_g, acc_u, y, r_sib, s1, r_x, s2, r_z,
            w_sem, ag_zs, ag_zr, ag_xs, ag_xr, ag_ss, ag_sr,
            rs_zs, rs_zr, rs_xs, rs_xr, rs_ss, rs_sr):
     nz, nx, widths, toks, quarters = cfg
@@ -74,7 +74,7 @@
     t = tok_ref[...].astype(F32)
     for j in range(chunks):
         parts = [t[:, lanes(q, j)] for q in range(quarters)]
-        x[j][core, xi, z] = jnp.concatenate(parts, axis=0).astype(BF16)
+        x[j][core, xi, z, :, :widths[j]] = jnp.concatenate(parts, axis=0).astype(BF16)
     rt = route_ref[...].astype(F32)
     gt = gate_ref[...]
     eye = lax.broadcasted_iota(jnp.int32, (toks, toks), 0) == lax.broadcasted_iota(jnp.int32, (toks, toks), 1)
@@ -88,12 +88,9 @@
     mid = (a - hi).astype(BF16).astype(F32)
     low = a - hi - mid
     terms = [hi, mid, low] + [jnp.zeros_like(a)] * (quarters - 3)
-    xa[core, xi, z] = jnp.concatenate(terms, axis=0).astype(BF16)
+    x[-1][core, xi, z, :, widths[-1]:] = jnp.concatenate(terms, axis=0).astype(BF16)
 
     pl.semaphore_wait(barrier, (nz - 1) + (nx - 1) + 1)
-
-    def buf(j):
-        return x[j] if j < chunks else xa
 
     def remote(src, dst, ss, rs, to):
         return pltpu.make_async_remote_copy(src_ref=src, dst_ref=dst, send_sem=ss, recv_sem=rs,
@@ -103,23 +100,23 @@
 
     def ag_z(j, i, incoming=False):
         at = lax.rem(z + nz - i, nz) if incoming else z
-        b = buf(j).at[core, :, at] if j == last else buf(j).at[core, xi, at]
+        b = x[j].at[core, :, at] if j == last else x[j].at[core, xi, at]
         return remote(b, b, ag_zs.at[j, i], ag_zr.at[j, i], dev(lax.rem(z + i, nz), xi, core))
 
     def ag_x(j, i, incoming=False):
         at = lax.rem(xi + nx - i, nx) if incoming else xi
-        b = buf(j).at[core, at, z] if j == last else buf(j).at[core, at]
+        b = x[j].at[core, at, z] if j == last else x[j].at[core, at]
         return remote(b, b, ag_xs.at[j, i], ag_xr.at[j, i], dev(z, lax.rem(xi + i, nx), core))
 
     def ag_s(j, incoming=False):
-        b = buf(j).at[1 - core if incoming else core]
+        b = x[j].at[1 - core if incoming else core]
         return remote(b, b, ag_ss.at[j], ag_sr.at[j], dev(z, xi, 1 - core))
 
     def hops(first, j):
         along_z = first != (j == last)
         return (ag_z, nz) if along_z else (ag_x, nx)
 
-    order = list(range(chunks)) + [chunks]
+    order = list(range(chunks))
     for j in order:
         fn, n = hops(True, j)
         for i in range(1, n):
@@ -139,10 +136,12 @@
         for c in load_w(j):
             c.wait()
         rows = pl.ds(starts[j], widths[j])
-        xc = jnp.concatenate([p.astype(BF16) for p in arrange(x[j], widths[j])], axis=1)
+        parts = arrange(x[j], x[j].shape[-1])
+        xc = jnp.concatenate([p[:, :widths[j]].astype(BF16) for p in parts], axis=1)
         for acc, wt in ((acc_g, wg), (acc_u, wu)):
             d = jnp.dot(xc, wt[:, rows, :].reshape(quarters * widths[j], hid), preferred_element_type=F32)
             acc[...] = d if j == 0 else acc[...] + d
+        return parts
 
     for j in [last] + [j for j in order if j != last]:
         fn, n = hops(True, j)
@@ -158,11 +157,10 @@
         ag_s(j).start()
     for j in order:
         ag_s(j, True).wait_recv()
-        if j < chunks:
-            gate_up(j)
+        parts = gate_up(j)
 
     own = lax.broadcasted_iota(jnp.int32, (ndev * toks, 128), 1) == z
-    aa = functools.reduce(lambda p, q: p + q, arrange(xa, 128)[:3])
+    aa = functools.reduce(lambda p, q: p + q, [p[:, widths[last]:] for p in parts[:3]])
     share = jnp.sum(jnp.where(own, aa, 0.0), axis=1, keepdims=True)
     g = acc_g[...]
     h = (g / (1.0 + jnp.exp(-g)) * acc_u[...]).astype(BF16)
@@ -275,8 +273,8 @@
     cfg = (nz, nx, widths, toks, quarters)
     dma = pltpu.SemaphoreType.DMA
 
-    def per_chunk(lead):
-        return [pltpu.VMEM(lead(j) + (ROWS, widths[j]), BF16) for j in range(chunks)]
+    def per_chunk(lead, extra=0):
+        return [pltpu.VMEM(lead(j) + (ROWS, widths[j] + (extra if j == last else 0)), BF16) for j in range(chunks)]
 
     vm = pl.BlockSpec(memory_space=pltpu.VMEM)
     hbm = pl.BlockSpec(memory_space=pl.ANY)
@@ -289,8 +287,7 @@
             pltpu.VMEM((quarters, quarter, hid), BF16),
             pltpu.VMEM((quarters, quarter, hid), BF16),
             pltpu.VMEM((hid, width), BF16),
-            per_chunk(lambda j: (2, nx, nz)),
-            pltpu.VMEM((2, nx, nz, ROWS, 128), BF16),
+            per_chunk(lambda j: (2, nx, nz), 128),
             pltpu.VMEM((ndev * toks, hid), F32),
             pltpu.VMEM((ndev * toks, hid), F32),
             per_chunk(lambda j: (2, nx, nz)),
@@ -300,9 +297,9 @@
             per_chunk(lambda j: (nx,) if j == last else (nz,)),
             per_chunk(lambda j: (nz, nx) if j == last else (nz,)),
             dma((3, max(chunks, quarters))),
-            dma((chunks + 1, nz)), dma((chunks + 1, nz)),
-            dma((chunks + 1, nx)), dma((chunks + 1, nx)),
-            dma((chunks + 1,)), dma((chunks + 1,)),
+            dma((chunks, nz)), dma((chunks, nz)),
+            dma((chunks, nx)), dma((chunks, nx)),
+            dma((chunks,)), dma((chunks,)),
             dma((chunks, nz)), dma((chunks, nz)),
             dma((chunks, nx)), dma((chunks, nx)),
             dma((chunks,)), dma((chunks,)),

time: 33.6 us -> 33.7 us (level)
  no operation moved by 1% of the time
where the time goes in v3:
time: 33.7 us; the launch traced here: 33.5 us
  Pallas kernels  32.1 us (95%)
  local copies, waits for them, and re-layouts  1.46 us (4%)
    pallas_call x1, Pallas kernels, on_device(): pl.pallas_call(functools.partial(kernel, cfg), out_shape=jax.ShapeDtypeSt...  32.1 us
    unnamed x1, local copies, waits for them, and re-layouts  1.46 us

profile of v3, /device:TPU:0, one launch (start us, length us, event | category | flops | bytes accessed | tf_op | source)
XLA Modules:
  0.0 33.5 jit_solution(17779211146449873186)
XLA Ops:
  0.0 32.1 %shard_map.64 = bf16[4,7168]{1,0:T(4,128)(2,1)} custom-call(bf16[4,7168]{1,0:T(4,128)(2,1)} %tok_ref.1, s32[2,4]{1,0:T(2,128)} %bitcast.8, f32[2,4]{1,0:T(2,128)} %bitcast.9, bf16[4,1792,512]{2,1,0:T(8,128)(2,1)} %bitcast.5, bf16[4,1792,512]{2,1,0:T(8,128)(2,1)} %bitcast.6, bf16[512,7168]{1,0:T(8,128)(2,1)} %bitcast.7), custom_call_target="tpu_custom_call" | custom-call | tf_op jit(solution)/shard_map/pallas_call | solution.py:281
  32.1 1.5 %copy.8 = bf16[4,7168]{1,0:T(4,128)(2,1)} copy(bf16[4,7168]{1,0:T(4,128)(2,1)} %shard_map.64) | data formatting | bytes 114688

commit v4 on v2

--- a/solution.py
+++ b/solution.py
@@ -56,12 +56,6 @@
         cols = pl.ds(q * quarter, quarter)
         return pltpu.make_async_copy(wd_hbm.at[:, cols], wd.at[:, cols], w_sem.at[2, q])
 
-    for j in range(chunks):
-        for c in load_w(j):
-            c.start()
-    for q in range(quarters):
-        load_d(q).start()
-
     barrier = pltpu.get_barrier_semaphore()
     zs = [lax.rem(z + i, nz) for i in range(1, nz)]
     xs = [lax.rem(xi + i, nx) for i in range(1, nx)]
@@ -70,6 +64,12 @@
     for xx in xs:
         pl.semaphore_signal(barrier, inc=1, device_id=dev(z, xx, core), device_id_type=pl.DeviceIdType.MESH)
     pl.semaphore_signal(barrier, inc=1, device_id=dev(z, xi, 1 - core), device_id_type=pl.DeviceIdType.MESH)
+
+    for j in range(chunks):
+        for c in load_w(j):
+            c.start()
+    for q in range(quarters):
+        load_d(q).start()
 
     t = tok_ref[...].astype(F32)
     for j in range(chunks):

time: 33.6 us -> 33.6 us (level)
  no operation moved by 1% of the time
where the time goes in v4:
time: 33.6 us; the launch traced here: 33.4 us
  Pallas kernels  31.9 us (95%)
  local copies, waits for them, and re-layouts  1.46 us (4%)
    pallas_call x1, Pallas kernels, on_device(): pl.pallas_call(functools.partial(kernel, cfg), out_shape=jax.ShapeDtypeSt...  31.9 us
    unnamed x1, local copies, waits for them, and re-layouts  1.46 us

profile of v4, /device:TPU:0, one launch (start us, length us, event | category | flops | bytes accessed | tf_op | source)
XLA Modules:
  0.0 33.4 jit_solution(5886671362920280028)
XLA Ops:
  0.0 31.9 %shard_map.64 = bf16[4,7168]{1,0:T(4,128)(2,1)} custom-call(bf16[4,7168]{1,0:T(4,128)(2,1)} %tok_ref.1, s32[2,4]{1,0:T(2,128)} %bitcast.8, f32[2,4]{1,0:T(2,128)} %bitcast.9, bf16[4,1792,512]{2,1,0:T(8,128)(2,1)} %bitcast.5, bf16[4,1792,512]{2,1,0:T(8,128)(2,1)} %bitcast.6, bf16[512,7168]{1,0:T(8,128)(2,1)} %bitcast.7), custom_call_target="tpu_custom_call" | custom-call | tf_op jit(solution)/shard_map/pallas_call | solution.py:283
  31.9 1.5 %copy.8 = bf16[4,7168]{1,0:T(4,128)(2,1)} copy(bf16[4,7168]{1,0:T(4,128)(2,1)} %shard_map.64) | data formatting | bytes 114688
